TPU v7x, 32 devices: a whole 2x2x4 slice. The times are simulated.
32 devices in a mesh: row: 4 (over z), col: 4 (over y, x), rep: 2 (over core).
Axes of the slice: x: 2, y: 2, z: 4, core: 2. Of those that a mesh axis runs over, the one named last changes fastest.
Arguments:
- amplitudes: bfloat16 [4096, 8192], P('row', ('rep', 'col')), may hold values from -6 to 6
- integrals: bfloat16 [8192, 4096], P(('rep', 'row'), 'col'), may hold values from -0.09375 to 0.09375
- tile_mask: int32 [64, 32], replicated, may hold values from 0 to 1
- k_irrep: int32 [64], replicated, may hold values from 0 to 3
- n_irrep: int32 [32], replicated, may hold values from 0 to 3
- stored_tile: int32 [64], replicated, may hold values from 0 to 63, as said below
Outputs:
- ladder: bfloat16 [4096, 4096], P('row', ('col', 'rep'))
Inputs may be any that keep to these rules, and one draw needn't show every extreme that they name: `stored_tile`: for each q, slots q * 32 to (q + 1) * 32 - 1 hold a permutation of the tiles q * 32 to (q + 1) * 32 - 1.
All inputs are finite; a program needn't handle non-finite values.
Results may differ from a plain program's by a relative error of at most 0.001.
Values may be sent and summed in bfloat16 or wider, within the bound.
A program may use at most 128 MiB of HBM per device.

v0:
```python
import jax
import jax.numpy as jnp
from jax import lax
from jax.sharding import PartitionSpec as P

TS = 128


def on_device(amplitudes, integrals, tile_mask, k_irrep, n_irrep, stored_tile):
    slab = lax.axis_index("rep")
    column = lax.axis_index("col")
    ncol = integrals.shape[1]
    tiles_col = ncol // TS
    n_labels = lax.dynamic_slice_in_dim(n_irrep, column * tiles_col, tiles_col)
    mask_cols = lax.dynamic_slice_in_dim(tile_mask, column * tiles_col, tiles_col, 1)
    stored_rows = integrals.shape[0]
    kq = stored_rows * lax.axis_size("row")
    slab_tiles = kq // TS
    slots = lax.dynamic_slice_in_dim(stored_tile, slab * slab_tiles, slab_tiles)
    gathered = lax.all_gather(integrals, "row", axis=0, tiled=True)
    same = jnp.take(k_irrep, slots)[:, None] == n_labels[None, :]
    occupied = jnp.take(mask_cols, slots, axis=0) == 1
    weights = jnp.logical_and(same, occupied).astype(jnp.bfloat16)
    shaped = gathered.reshape(slab_tiles, TS, tiles_col, TS) * weights[:, None, :, None]
    masked = shaped.reshape(kq, ncol)
    amp_slab = lax.all_gather(amplitudes, "col", axis=1, tiled=True)
    mrow = amp_slab.shape[0]
    local_ids = slots - slab * slab_tiles
    ordered = jnp.take(amp_slab.reshape(mrow, slab_tiles, TS), local_ids, axis=1).reshape(mrow, kq)
    partial_value = jnp.dot(ordered, masked, preferred_element_type=jnp.float32)
    return lax.psum_scatter(partial_value, "rep", scatter_dimension=1, tiled=True).astype(
        jnp.bfloat16
    )


def solution(mesh):
    placed = (P("row", ("rep", "col")), P(("rep", "row"), "col"), P(), P(), P(), P())
    return jax.shard_map(
        on_device, mesh=mesh, in_specs=placed, out_specs=P("row", ("col", "rep")), check_vma=False
    )
```

profile of v0, /device:TPU:0, one launch (start us, length us, event | category | flops | bytes accessed | tf_op | source)
XLA Modules:
  0.0 288.3 jit_solution(4569055873075597321)
XLA Ops:
  6.5 0.0 copy-start
  6.5 0.0 copy-start.5
  6.5 0.0 copy-start.4
  6.5 0.0 copy-start.2
  6.5 0.0 all-gather.3.cloned.1.call-start
  6.6 3.9 %copy.13 = bf16[1024,1024]{0,1:T(8,128)(2,1)} copy(bf16[1024,1024]{1,0:T(8,128)(2,1)} %param.6) | data formatting | bytes 4194304 | tf_op args[0]
  10.5 0.0 all-gather.3.cloned.1.call-update
  10.6 0.0 all-gather.5.cloned.1.call-start
  10.6 0.7 all-gather.5.cloned.1.call-update
  11.3 0.0 reduce-scatter.2.cloned.1.call-start
  11.4 0.0 copy-done.5
  11.4 0.1 dynamic_slice.10
  11.4 0.0 copy-done
  11.4 0.1 copy.19
  11.5 0.0 copy-done.4
  11.5 0.1 compare_and_fusion
  11.6 0.0 copy-done.2
  11.6 0.7 gather_fusion.1
  12.3 0.6 gather_fusion.2
  12.9 0.1 copy.17
  13.0 0.1 fusion.3
  13.1 0.1 copy.18
  13.2 0.1 broadcast_bitcast_fusion
  13.2 87.8 %all-gather.3.cloned.1.call-done = bf16[1024,4096]{0,1:T(8,128)(2,1)} async-done(((bf16[1024,1024]{0,1:T(8,128)(2,1)}), bf16[1024,4096]{0,1:T(8,128)(2,1)}) %all-gather.3.cloned.1.call-update) | async-done | bytes 8388624 | tf_op jit(solution)/shard_map/all_gather | solution.py:26
  101.0 12.1 %copy.14 = bf16[1024,32,128]{2,0,1:T(8,128)(2,1)} copy(bf16[1024,32,128]{0,2,1:T(8,128)(2,1)} %bitcast.14) | data formatting | bytes 16777216 | tf_op jit(solution)/shard_map/reshape | solution.py:29
  113.1 9.1 %gather_fusion = bf16[32,1024,128]{2,1,0:T(8,128)(2,1)} fusion(bf16[1024,32,128]{2,0,1:T(8,128)(2,1)} %copy.14, s32[1024]{0:T(1024)S(1)} %pad_clamp_fusion.1), kind=kCustom, calls=%fused_computation | custom fusion | bytes 16777344 | tf_op jit(solution)/shard_map/jit(_take)/gather | solution.py:29
  122.2 12.0 %copy.15 = bf16[1024,32,128]{0,2,1:T(8,128)(2,1)} copy(bf16[1024,32,128]{2,0,1:T(8,128)(2,1)} %bitcast.12) | data formatting | bytes 16777216 | tf_op jit(solution)/shard_map/jit(_take)/gather | solution.py:29
  134.2 7.3 %bitcast_select_fusion = bf16[1024,4096]{0,1:T(8,128)(2,1)} fusion(bf16[1024,32,128]{0,2,1:T(8,128)(2,1)} %copy.15, pred[4096]{0:T(1024)(128)(4,1)S(1)} %broadcast_bitcast_fusion), kind=kLoop, calls=%fused_computation.6 | loop fusion | flops 4194304 | bytes 16781312 | tf_op jit(solution)/shard_map/jit(_take)/select_n | solution.py:29
  141.5 110.8 %all-gather.5.cloned.1.call-done = bf16[4096,1024]{1,0:T(8,128)(2,1)} async-done(((bf16[1024,1024]{1,0:T(8,128)(2,1)}), bf16[4096,1024]{1,0:T(8,128)(2,1)}) %all-gather.5.cloned.1.call-update) | async-done | bytes 8388624 | tf_op jit(solution)/shard_map/all_gather | solution.py:20
  252.3 0.0 copy-start.3
  252.3 1.1 mul.21
  253.4 2.2 copy-done.3
  255.6 0.0 copy-start.1
  255.6 12.9 %fusion = f32[1024,1024]{1,0:T(8,128)} fusion(bf16[1024,4096]{0,1:T(8,128)(2,1)S(1)} %copy-done.3, bf16[4096,1024]{1,0:T(8,128)(2,1)} %all-gather.5.cloned.1.call-done, bf16[512,8,8,128]{3,2,1,0:T(8,128)(2,1)S(1)} %bitcast.13), kind=kOutput, calls=%fused_computation.4 | convolution fusion | flops 8594128896 | bytes 29360128 | tf_op jit(solution)/shard_map/dot_general | solution.py:30
  268.6 0.0 reduce-scatter.2.cloned.1.call-update
  268.6 10.4 %reduce-scatter.2.cloned.1.call-done = f32[1024,512]{1,0:T(8,128)} async-done(((f32[1024,1024]{1,0:T(8,128)}), f32[1024,512]{1,0:T(8,128)}) %reduce-scatter.2.cloned.1.call-update) | async-done | bytes 2097168 | tf_op jit(solution)/shard_map/reduce_scatter | solution.py:31
  279.0 2.7 convert_element_type.11
  281.7 0.0 copy-done.1
  (4 shorter events, 0.0 us)
Async XLA Ops:
  6.5 4.9 %copy-start = (s32[64,32]{0,1:T(8,128)S(1)}, s32[64,32]{0,1:T(8,128)}, u32[]{:S(2)}) copy-start(s32[64,32]{0,1:T(8,128)} %param.8) | copy-start | bytes 24580
  6.5 4.8 %copy-start.5 = (s32[32]{0:T(128)S(1)}, s32[32]{0:T(128)}, u32[]{:S(2)}) copy-start(s32[32]{0:T(128)} %param.10) | copy-start | bytes 388
  6.5 5.0 %copy-start.4 = (s32[64]{0:T(128)S(1)}, s32[64]{0:T(128)}, u32[]{:S(2)}) copy-start(s32[64]{0:T(128)} %param.11) | copy-start | bytes 772
  6.5 5.1 %copy-start.2 = (s32[64]{0:T(128)S(1)}, s32[64]{0:T(128)}, u32[]{:S(2)}) copy-start(s32[64]{0:T(128)} %param.9) | copy-start | bytes 772
  6.5 94.5 %all-gather.3.cloned.1.call-start = ((), (), s32[]{:S(2)}) async-start(), calls=%async_computation.1 | async-start | bytes 10485760 | tf_op jit(solution)/shard_map/all_gather | solution.py:26
  10.6 241.7 %all-gather.5.cloned.1.call-start = ((), (), s32[]{:S(2)}) async-start(), calls=%async_computation.2 | async-start | bytes 10485760 | tf_op jit(solution)/shard_map/all_gather | solution.py:20
  11.3 267.7 %reduce-scatter.2.cloned.1.call-start = ((), (), s32[]{:S(2)}) async-start(), calls=%async_computation.3 | async-start | bytes 6291456 | tf_op jit(solution)/shard_map/reduce_scatter | solution.py:31
  252.3 3.4 %copy-start.3 = (bf16[1024,4096]{0,1:T(8,128)(2,1)S(1)}, bf16[1024,4096]{0,1:T(8,128)(2,1)}, u32[]{:S(2)}) copy-start(bf16[1024,4096]{0,1:T(8,128)(2,1)} %bitcast_select_fusion) | copy-start | bytes 25165828
  255.6 26.1 %copy-start.1 = (s32[64,32]{0,1:T(8,128)S(1)}, s32[64,32]{0,1:T(8,128)}, u32[]{:S(2)}) copy-start(s32[64,32]{0,1:T(8,128)} %param.8) | copy-start | bytes 24580
Sparse Core Ops, SparseCore 0:
  10.7 90.2 all-gather.2
  102.6 149.6 all-gather.4
  268.7 10.2 reduce-scatter.1
where the time goes:
time: 289 us; the launch traced here: 288 us
  waiting for transfers between devices  210 us (73%)
  local copies, waits for them, and re-layouts  42.2 us (15%)
  between operations  13.2 us (5%)
  matrix products  12.9 us (4%)
  other arithmetic  10.2 us (4%)
    all_gather x1, waiting for transfers between devices, on_device(): gathered = lax.all_gather(integrals, 'row', axis=0, tiled=True)  111 us
    all_gather x1, waiting for transfers between devices, on_device(): amp_slab = lax.all_gather(amplitudes, 'col', axis=1, tiled=True)  87.8 us
    gather x2, local copies, waits for them, and re-layouts, on_device(): jnp.take(amp_slab.reshape(mrow, slab_tiles, TS), local_ids, axis=1)  21.1 us
    dot_general x1, matrix products, on_device(): partial_value = jnp.dot(ordered, masked, preferred_element_type=jnp.float32)  12.9 us
    reshape x1, local copies, waits for them, and re-layouts, on_device(): amp_slab.reshape(mrow, slab_tiles, TS)  12.1 us
    reduce_scatter x1, waiting for transfers between devices, on_device(): lax.psum_scatter(partial_value, 'rep', scatter_dimension=1, tiled=True)  10.4 us
    select_n x1, other arithmetic, on_device(): jnp.take(amp_slab.reshape(mrow, slab_tiles, TS), local_ids, axis=1)  7.3 us
    unnamed x14, local copies, waits for them, and re-layouts  6.28 us
  transfers between devices with their start and end apart: 3, of which 3 were waited for; matrix products, arithmetic and copies ran while one was open for 15% of the time, Pallas kernels for 0%

commit v1 on v0

v1 whole, which is shorter than its diff:
```python
import functools

import jax
import jax.numpy as jnp
from jax import lax
from jax.experimental import pallas as pl
from jax.experimental.pallas import tpu as pltpu
from jax.sharding import PartitionSpec as P

TS = 128
PARTS = 4


def remote(src, dst, send_sem, recv_sem, **target):
    return pltpu.make_async_remote_copy(
        src_ref=src,
        dst_ref=dst,
        send_sem=send_sem,
        recv_sem=recv_sem,
        device_id=target,
        device_id_type=pl.DeviceIdType.MESH,
    )


def kernel(
    a_ref,
    b_ref,
    mask_ref,
    k_ref,
    n_ref,
    stored_ref,
    out_ref,
    a_0,
    a_1,
    a_2,
    a_3,
    a_ord,
    a_far,
    b_all,
    part_out,
    part_in,
    fp_out,
    f_in,
    f_out,
    own_sem,
    a_send,
    a_recv,
    b_send,
    b_recv,
    far_send,
    far_recv,
    fp_send,
    fp_recv,
    f_send,
    f_recv,
    p_send,
    p_recv,
):
    a_all = (a_0, a_1, a_2, a_3)
    z = lax.axis_index("row")
    c = lax.axis_index("col")
    r = lax.axis_index("rep")
    rows_n = b_all.shape[0]
    end = jnp.logical_or(z == 0, z == rows_n - 1)
    inner = jnp.logical_not(end)
    near = 2 * (z // 2)
    far = 2 - near
    buddy = z + 1 - 2 * (z % 2)
    across = rows_n - 1 - z
    beyond = rows_n - 1 - buddy
    x = c % 2
    y = c // 2
    xn = y * 2 + (1 - x)
    yn = (1 - y) * 2 + x
    diag = (1 - y) * 2 + (1 - x)
    mrow, kcol = a_ref.shape
    kb, ncol = b_ref.shape
    half = ncol // 2
    slots = kb // TS
    slab_tiles = slots * rows_n
    per = kcol // TS
    ra = mrow // PARTS
    steps = half // TS
    mesh_id = pl.DeviceIdType.MESH

    own = [
        pltpu.make_async_copy(
            a_ref.at[pl.ds(i * ra, ra), pl.ds(t * TS, TS)],
            a_all[i].at[c * per + t],
            own_sem.at[i, t],
        )
        for i in range(PARTS)
        for t in range(per)
    ]
    for copy in own:
        copy.start()

    barrier = pltpu.get_barrier_semaphore()
    pl.semaphore_signal(barrier, inc=1, device_id={"col": xn}, device_id_type=mesh_id)
    pl.semaphore_signal(barrier, inc=1, device_id={"col": yn}, device_id_type=mesh_id)
    pl.semaphore_signal(barrier, inc=1, device_id={"rep": 1 - r}, device_id_type=mesh_id)
    pl.semaphore_signal(barrier, inc=1, device_id={"row": buddy}, device_id_type=mesh_id)

    @pl.when(inner)
    def _():
        pl.semaphore_signal(barrier, inc=1, device_id={"row": across}, device_id_type=mesh_id)

    pl.semaphore_wait(barrier, 4 + jnp.where(inner, 1, 0))

    for copy in own:
        copy.wait()

    def rows(i):
        return pl.ds(i * ra, ra)

    def a_copy(kind, i, receive=False):
        link = kind % 2
        if kind < 2:
            owner = (xn, yn)[link] if receive else c
            view = a_all[i].at[pl.ds(owner * per, per)]
        else:
            owner = diag if receive else (yn, xn)[link]
            part = pl.ds(link * (ra // 2), ra // 2)
            view = a_all[i].at[pl.ds(owner * per, per), part, :]
        return remote(view, view, a_send.at[kind, i], a_recv.at[kind, i], col=(xn, yn)[link])

    def a_own(i):
        if i < PARTS:
            a_copy(0, i).start()
            a_copy(1, i).start()

    def a_pass(i):
        a_copy(0, i, True).wait_recv()
        a_copy(3, i).start()
        a_copy(1, i, True).wait_recv()
        a_copy(2, i).start()

    def a_done(i):
        a_copy(2, i, True).wait_recv()
        a_copy(3, i, True).wait_recv()

    def tile_of(j):
        p = j // 2
        return ((1 - r) if j % 2 == 0 else r) * steps + p

    def lanes(t):
        return pl.ds(pl.multiple_of(t * TS, TS), TS)

    def b_copy(kind, j, receive=False):
        if receive:
            owner = (buddy, across, beyond)[kind]
        else:
            owner = (z, z, buddy)[kind]
        view = b_all.at[owner, :, lanes(tile_of(j))]
        target = buddy if kind == 0 else across
        return remote(view, view, b_send.at[kind, j], b_recv.at[kind, j], row=target)

    def far_copy(kind, i, receive=False):
        side = x if i % 2 == 0 else y
        if kind == 0:
            src = a_far if receive else a_ord
            first = 0 if receive else far
            return remote(
                src.at[first + side, rows(i), :],
                a_far.at[side, rows(i), :],
                far_send.at[0, i],
                far_recv.at[0, i],
                row=buddy,
            )
        view = a_far.at[(1 - side) if receive else side, rows(i), :]
        return remote(
            view, view, far_send.at[1, i], far_recv.at[1, i], col=xn if i % 2 == 0 else yn
        )

    def fp_copy(i, p):
        return remote(
            fp_out.at[i, p], f_in.at[i, p], fp_send.at[i, p], fp_recv.at[i, p], rep=1 - r
        )

    def f_copy(i, p):
        return remote(
            f_out.at[i, p], f_in.at[i, p], f_send.at[i, p], f_recv.at[i, p], row=buddy
        )

    def swap():
        return remote(part_out, part_in, p_send.at[0], p_recv.at[0], rep=1 - r)

    def order(block, i):
        def one(s, carry):
            t = jnp.maximum(stored_ref[r * slab_tiles + block * slots + s] - r * slab_tiles, 0)
            a_ord[block, rows(i), lanes(s)] = a_all[i][t]
            return carry

        lax.fori_loop(0, slots, one, 0)

    def mask(j):
        tile = tile_of(j)
        g = c * (ncol // TS) + tile

        def one(t, carry):
            k = stored_ref[r * slab_tiles + z * slots + t]
            ok = jnp.logical_and(k_ref[k] == n_ref[g], mask_ref[k, g] == 1)
            weight = jnp.where(ok, 1.0, 0.0).astype(jnp.float32)
            at = pl.ds(pl.multiple_of(t * TS, TS), TS)
            value = b_ref[at, lanes(tile)].astype(jnp.float32) * weight
            b_all[z, at, lanes(tile)] = value.astype(jnp.bfloat16)
            return carry

        lax.fori_loop(0, slots, one, 0)

    def product(first, count, side):
        cols = pl.ds(pl.multiple_of(side * half, half), half)

        def one(i):
            at = pl.ds(pl.multiple_of(i * ra, ra), ra)
            total = jnp.zeros((ra, half), jnp.float32)
            for s in range(count):
                total += jnp.dot(
                    a_ord[first + s, at, :],
                    b_all[first + s, :, cols],
                    preferred_element_type=jnp.float32,
                )
            return at, total

        return one

    def send_partial(first, count):
        part = product(first, count, 1 - r)

        def away(i, carry):
            at, total = part(i)
            part_out[at, :] = total
            return carry

        lax.fori_loop(0, PARTS, away, 0)
        swap().start()

    def far_dot(i, j):
        total = jnp.zeros((ra, TS), jnp.float32)
        for s in range(2):
            total += jnp.dot(
                a_far[s, rows(i), :],
                b_all[far + s, :, lanes(tile_of(j))],
                preferred_element_type=jnp.float32,
            )
        return total

    def far_steps(pairs):
        for i, p in pairs:
            fp_out[i, p] = far_dot(i, 2 * p)
            fp_copy(i, p).start()
        for i, p in pairs:
            total = far_dot(i, 2 * p + 1)
            fp_copy(i, p).wait_recv()
            f_out[i, p] = total + f_in[i, p]
            f_copy(i, p).start()

    a_own(0)
    a_own(1)
    chunks = 2 * steps

    @pl.when(end)
    def _():
        for j in range(chunks):
            mask(j)
            if j < PARTS:
                b_copy(0, j).start()
        sent = PARTS
        for i in range(PARTS):
            a_pass(i)
            a_own(i + 2)
            a_done(i)
            side = x if i % 2 == 0 else y
            order(far + side, i)
            far_copy(0, i).start()
            more = (0, 2, 1, chunks)[i]
            for j in range(sent, min(chunks, sent + more)):
                b_copy(0, j).start()
            sent = min(chunks, sent + more)
        for i in range(PARTS):
            order(near, i)
            order(near + 1, i)
        for j in range(chunks):
            b_copy(0, j, True).wait_recv()
        send_partial(near, 2)
        part = product(near, 2, r)

        def stay(i, carry):
            at, total = part(i)
            for p in range(steps):
                f_out[i, p] = total[:, p * TS : (p + 1) * TS]
            return carry

        lax.fori_loop(0, PARTS, stay, 0)
        swap().wait_recv()
        for i, p in FAR_ORDER:
            f_copy(i, p).wait_recv()
            cols = pl.ds(p * TS, TS)
            value = f_out[i, p] + part_in[rows(i), cols] + f_in[i, p]
            out_ref[rows(i), cols] = value.astype(jnp.bfloat16)
        for i in range(PARTS):
            far_copy(0, i).wait_send()

    @pl.when(inner)
    def _():
        def pass_b(j):
            b_copy(1, j).start()
            b_copy(0, j, True).wait_recv()
            b_copy(2, j).start()

        def far_pass(i):
            far_copy(0, i, True).wait_recv()
            far_copy(1, i).start()

        def far_b(p):
            for j in (2 * p, 2 * p + 1):
                b_copy(1, j, True).wait_recv()
                b_copy(2, j, True).wait_recv()

        for j in range(chunks):
            mask(j)
            b_copy(0, j).start()
        pass_b(0)
        pass_b(1)
        a_pass(0)
        a_own(2)
        pass_b(2)
        pass_b(3)
        a_pass(1)
        a_own(3)
        far_pass(0)
        far_pass(1)
        a_pass(2)
        pass_b(4)
        pass_b(5)
        far_copy(1, 0, True).wait_recv()
        far_copy(1, 1, True).wait_recv()
        far_b(0)
        far_b(1)
        far_steps(FAR_ORDER[0:4])
        a_pass(3)
        far_pass(2)
        pass_b(6)
        far_b(2)
        far_steps(FAR_ORDER[4:6])
        far_pass(3)
        pass_b(7)
        far_copy(1, 2, True).wait_recv()
        far_steps(FAR_ORDER[6:9])
        far_copy(1, 3, True).wait_recv()
        far_steps(FAR_ORDER[9:12])
        far_b(3)
        far_steps(FAR_ORDER[12:16])
        for i in range(PARTS):
            a_done(i)
            for s in range(rows_n):
                order(s, i)
        send_partial(0, rows_n)
        part = product(0, rows_n, r)

        def keep(i, carry):
            at, total = part(i)
            for p in range(steps):
                fp_out[i, p] = total[:, p * TS : (p + 1) * TS]
            return carry

        for i, p in FAR_ORDER:
            fp_copy(i, p).wait_send()
        lax.fori_loop(0, PARTS, keep, 0)
        swap().wait_recv()

        def stay(i, carry):
            at = pl.ds(pl.multiple_of(i * ra, ra), ra)
            for p in range(steps):
                cols = pl.ds(p * TS, TS)
                out_ref[at, cols] = (fp_out[i, p] + part_in[at, cols]).astype(jnp.bfloat16)
            return carry

        lax.fori_loop(0, PARTS, stay, 0)
        for i, p in FAR_ORDER:
            f_copy(i, p).wait_send()
        for i in range(PARTS):
            far_copy(1, i).wait_send()
        for j in range(chunks):
            b_copy(1, j).wait_send()
            b_copy(2, j).wait_send()

    swap().wait_send()
    for i in range(PARTS):
        for kind in range(4):
            a_copy(kind, i).wait_send()
    for j in range(chunks):
        b_copy(0, j).wait_send()


FAR_ORDER = (
    (0, 0), (1, 0), (0, 1), (1, 1),
    (0, 2), (1, 2),
    (2, 0), (2, 1), (2, 2),
    (3, 0), (3, 1), (3, 2),
    (0, 3), (1, 3), (2, 3), (3, 3),
)


def fused(rows_n, cols_n, amplitudes, integrals, tile_mask, k_irrep, n_irrep, stored_tile):
    mrow, kcol = amplitudes.shape
    kb, ncol = integrals.shape
    half = ncol // 2
    steps = half // TS
    smem = pl.BlockSpec(memory_space=pltpu.SMEM)
    vmem = pl.BlockSpec(memory_space=pltpu.VMEM)
    tiles = pltpu.VMEM((PARTS, steps, mrow // PARTS, TS), jnp.float32)
    chunk = pltpu.VMEM((cols_n * kcol // TS, mrow // PARTS, TS), jnp.bfloat16)
    dma = pltpu.SemaphoreType.DMA
    return pl.pallas_call(
        kernel,
        out_shape=jax.ShapeDtypeStruct((mrow, half), jnp.bfloat16),
        in_specs=[pl.BlockSpec(memory_space=pl.ANY), vmem, smem, smem, smem, smem],
        out_specs=vmem,
        scratch_shapes=[
            chunk,
            chunk,
            chunk,
            chunk,
            pltpu.VMEM((rows_n, mrow, kb), jnp.bfloat16),
            pltpu.VMEM((2, mrow, kb), jnp.bfloat16),
            pltpu.VMEM((rows_n, kb, ncol), jnp.bfloat16),
            pltpu.VMEM((mrow, half), jnp.float32),
            pltpu.VMEM((mrow, half), jnp.float32),
            tiles,
            tiles,
            tiles,
            dma((PARTS, kcol // TS)),
            dma((4, PARTS)),
            dma((4, PARTS)),
            dma((3, 2 * steps)),
            dma((3, 2 * steps)),
            dma((2, PARTS)),
            dma((2, PARTS)),
            dma((PARTS, steps)),
            dma((PARTS, steps)),
            dma((PARTS, steps)),
            dma((PARTS, steps)),
            dma((1,)),
            dma((1,)),
        ],
        compiler_params=pltpu.CompilerParams(
            collective_id=0, has_side_effects=True, vmem_limit_bytes=56 << 20
        ),
        cost_estimate=pl.CostEstimate(
            flops=2 * mrow * kb * rows_n * ncol,
            bytes_accessed=2 * (mrow * kcol + kb * ncol + mrow * half),
            transcendentals=0,
        ),
    )(amplitudes, integrals, tile_mask, k_irrep, n_irrep, stored_tile)


def gathered_form(amplitudes, integrals, tile_mask, k_irrep, n_irrep, stored_tile):
    slab = lax.axis_index("rep")
    column = lax.axis_index("col")
    place = lax.axis_index("row")
    kb, ncol = integrals.shape
    tiles_col = ncol // TS
    own = kb // TS
    slab_tiles = own * lax.axis_size("row")
    n_labels = lax.dynamic_slice_in_dim(n_irrep, column * tiles_col, tiles_col)
    mask_cols = lax.dynamic_slice_in_dim(tile_mask, column * tiles_col, tiles_col, 1)
    slots = lax.dynamic_slice_in_dim(stored_tile, slab * slab_tiles, slab_tiles)
    mine = lax.dynamic_slice_in_dim(slots, place * own, own)
    same = jnp.take(k_irrep, mine)[:, None] == n_labels[None, :]
    weights = jnp.logical_and(same, jnp.take(mask_cols, mine, axis=0) == 1).astype(jnp.bfloat16)
    shaped = integrals.reshape(own, TS, tiles_col, TS) * weights[:, None, :, None]
    masked = lax.all_gather(shaped.reshape(kb, ncol), "row", axis=0, tiled=True)
    amp_slab = lax.all_gather(amplitudes, "col", axis=1, tiled=True)
    mrow, kq = amp_slab.shape
    ordered = jnp.take(
        amp_slab.reshape(mrow, slab_tiles, TS), slots - slab * slab_tiles, axis=1
    ).reshape(mrow, kq)
    partial_value = jnp.dot(ordered, masked, preferred_element_type=jnp.float32)
    return lax.psum_scatter(partial_value, "rep", scatter_dimension=1, tiled=True).astype(
        jnp.bfloat16
    )


def solution(mesh):
    rows_n, cols_n, reps = (mesh.shape[name] for name in ("row", "col", "rep"))
    if (rows_n, cols_n, reps) == (4, 4, 2):
        body = functools.partial(fused, rows_n, cols_n)
    else:
        body = gathered_form
    placed = (P("row", ("rep", "col")), P(("rep", "row"), "col"), P(), P(), P(), P())
    return jax.shard_map(
        body, mesh=mesh, in_specs=placed, out_specs=P("row", ("col", "rep")), check_vma=False
    )
```

time: 289 us -> 148 us (0.51)
  waiting for transfers between devices: 210 us -> 0 us
  Pallas kernels: 0 us -> 144 us
  local copies, waits for them, and re-layouts: 42.2 us -> 3.68 us
  between operations: 13.2 us -> 0.01 us
  matrix products: 12.9 us -> 0 us
  other arithmetic: 10.2 us -> 0 us
    all_gather x2 -> x0, waiting for transfers between devices: 199 us -> none  [the longest x1 111 us: on_device(): gathered = lax.all_gather(integrals, 'row', axis=0, tiled=True)]
    pallas_call x0 -> x1, Pallas kernels: none -> 144 us  [fused(): pl.pallas_call(kernel, out_shape=jax.ShapeDtypeStruct((mrow, half), jnp.b...]
    gather x5 -> x0, local copies, waits for them, and re-layouts: 22.4 us -> none  [the longest x2 21.1 us: on_device(): jnp.take(amp_slab.reshape(mrow, slab_tiles, TS), local_ids, axis=1)]
    dot_general x1 -> x0, matrix products: 12.9 us -> none  [on_device(): partial_value = jnp.dot(ordered, masked, preferred_element_type=jnp.float32)]
    reshape x1 -> x0, local copies, waits for them, and re-layouts: 12.1 us -> none  [on_device(): amp_slab.reshape(mrow, slab_tiles, TS)]
    reduce_scatter x1 -> x0, waiting for transfers between devices: 10.4 us -> none  [on_device(): lax.psum_scatter(partial_value, 'rep', scatter_dimension=1, tiled=True)]
    select_n x2 -> x0, other arithmetic: 7.31 us -> none  [the longest x1 7.3 us: on_device(): jnp.take(amp_slab.reshape(mrow, slab_tiles, TS), local_ids, axis=1)]
    unnamed x14 -> x2, local copies, waits for them, and re-layouts: 6.28 us -> 3.68 us
  transfers between devices with their start and end apart: 3 -> 0, of which waited for: 3 -> 0; matrix products, arithmetic and copies ran while one was open for 15% -> 0% of each run, Pallas kernels for 0% -> 0%
where the time goes in v1:
time: 148 us
  Pallas kernels  144 us (97%)
  local copies, waits for them, and re-layouts  3.68 us (2%)
    pallas_call x1, Pallas kernels, fused(): pl.pallas_call(kernel, out_shape=jax.ShapeDtypeStruct((mrow, half), jnp.b...  144 us
    unnamed x2, local copies, waits for them, and re-layouts  3.68 us

profile of v1, /device:TPU:0, one launch (start us, length us, event | category | flops | bytes accessed | tf_op | source)
XLA Modules:
  0.0 147.7 jit_solution(16205044844855212595)
XLA Ops:
  0.0 1.4 copy.7.mask_ref
  1.4 144.0 %shard_map.64 = bf16[1024,512]{1,0:T(8,128)(2,1)} custom-call(bf16[1024,1024]{1,0:T(8,128)(2,1)} %a_ref.1, bf16[1024,1024]{1,0:T(8,128)(2,1)} %b_ref.1, s32[64,32]{1,0:T(8,128)} %copy.7.mask_ref, s32[64]{0:T(128)} %k_ref.1, s32[32]{0:T(128)} %n_ref.1, s32[64]{0:T(128)} %stored_ref.1), custom_call_target="tpu_custom_call" | custom-call | flops 8589934592 | bytes 5242880 | tf_op jit(solution)/shard_map/pallas_call | solution.py:415
  145.5 2.3 %copy.9 = bf16[1024,512]{1,0:T(8,128)(2,1)} copy(bf16[1024,512]{1,0:T(8,128)(2,1)} %shard_map.64) | data formatting | bytes 2097152

commit v2 on v1

--- a/solution.py
+++ b/solution.py
@@ -81,6 +81,7 @@
     per = kcol // TS
     ra = mrow // PARTS
     steps = half // TS
+    wide = half // 2
     mesh_id = pl.DeviceIdType.MESH
 
     own = [
@@ -148,28 +149,23 @@
 
     def b_copy(kind, j, receive=False):
         if receive:
-            owner = (buddy, across, beyond)[kind]
+            owner = (buddy, across, beyond, beyond, across)[kind]
         else:
-            owner = (z, z, buddy)[kind]
+            owner = (z, z, buddy, across, beyond)[kind]
         view = b_all.at[owner, :, lanes(tile_of(j))]
-        target = buddy if kind == 0 else across
+        target = across if kind in (1, 2) else buddy
         return remote(view, view, b_send.at[kind, j], b_recv.at[kind, j], row=target)
 
-    def far_copy(kind, i, receive=False):
-        side = x if i % 2 == 0 else y
+    def far_copy(kind, i, h, receive=False):
+        side = (x, y)[h]
+        at = pl.ds(i * ra + h * (ra // 2), ra // 2)
         if kind == 0:
-            src = a_far if receive else a_ord
-            first = 0 if receive else far
-            return remote(
-                src.at[first + side, rows(i), :],
-                a_far.at[side, rows(i), :],
-                far_send.at[0, i],
-                far_recv.at[0, i],
-                row=buddy,
-            )
-        view = a_far.at[(1 - side) if receive else side, rows(i), :]
+            src = a_far.at[side, at, :] if receive else a_ord.at[far + side, at, :]
+            dst = a_far.at[side, at, :]
+            return remote(src, dst, far_send.at[0, i, h], far_recv.at[0, i, h], row=buddy)
+        view = a_far.at[(1 - side) if receive else side, at, :]
         return remote(
-            view, view, far_send.at[1, i], far_recv.at[1, i], col=xn if i % 2 == 0 else yn
+            view, view, far_send.at[1, i, h], far_recv.at[1, i, h], col=(xn, yn)[h]
         )
 
     def fp_copy(i, p):
@@ -182,8 +178,8 @@
             f_out.at[i, p], f_in.at[i, p], f_send.at[i, p], f_recv.at[i, p], row=buddy
         )
 
-    def swap():
-        return remote(part_out, part_in, p_send.at[0], p_recv.at[0], rep=1 - r)
+    def swap(h):
+        return remote(part_out.at[h], part_in.at[h], p_send.at[h], p_recv.at[h], rep=1 - r)
 
     def order(block, i):
         def one(s, carry):
@@ -208,32 +204,41 @@
 
         lax.fori_loop(0, slots, one, 0)
 
-    def product(first, count, side):
-        cols = pl.ds(pl.multiple_of(side * half, half), half)
+    def product(first, count, side, h, extra=False):
+        cols = pl.ds(pl.multiple_of(side * half + h * wide, wide), wide)
 
         def one(i):
             at = pl.ds(pl.multiple_of(i * ra, ra), ra)
-            total = jnp.zeros((ra, half), jnp.float32)
+            total = jnp.zeros((ra, wide), jnp.float32)
             for s in range(count):
                 total += jnp.dot(
                     a_ord[first + s, at, :],
                     b_all[first + s, :, cols],
                     preferred_element_type=jnp.float32,
                 )
-            return at, total
+            if not extra:
+                return at, total
+            more = jnp.zeros((ra, TS), jnp.float32)
+            for s in range(2):
+                more += jnp.dot(
+                    a_ord[far + s, at, :],
+                    b_all[far + s, :, lanes(side * steps)],
+                    preferred_element_type=jnp.float32,
+                )
+            return at, jnp.concatenate([total[:, :TS] + more, total[:, TS:]], axis=1)
 
         return one
 
-    def send_partial(first, count):
-        part = product(first, count, 1 - r)
+    def send_partial(first, count, h, extra=False):
+        part = product(first, count, 1 - r, h, extra)
 
         def away(i, carry):
             at, total = part(i)
-            part_out[at, :] = total
+            part_out[h, at, :] = total
             return carry
 
         lax.fori_loop(0, PARTS, away, 0)
-        swap().start()
+        swap(h).start()
 
     def far_dot(i, j):
         total = jnp.zeros((ra, TS), jnp.float32)
@@ -261,45 +266,60 @@
 
     @pl.when(end)
     def _():
+        sent = PARTS + 1
         for j in range(chunks):
             mask(j)
-            if j < PARTS:
+            if j < sent:
                 b_copy(0, j).start()
-        sent = PARTS
         for i in range(PARTS):
             a_pass(i)
             a_own(i + 2)
             a_done(i)
-            side = x if i % 2 == 0 else y
-            order(far + side, i)
-            far_copy(0, i).start()
-            more = (0, 2, 1, chunks)[i]
-            for j in range(sent, min(chunks, sent + more)):
+            order(far, i)
+            order(far + 1, i)
+            for h in range(2):
+                far_copy(0, i, h).start()
+            upto = min(chunks, sent + i + 1)
+            for j in range(sent, upto):
                 b_copy(0, j).start()
-            sent = min(chunks, sent + more)
+            sent = upto
         for i in range(PARTS):
             order(near, i)
             order(near + 1, i)
         for j in range(chunks):
             b_copy(0, j, True).wait_recv()
-        send_partial(near, 2)
-        part = product(near, 2, r)
-
-        def stay(i, carry):
-            at, total = part(i)
-            for p in range(steps):
-                f_out[i, p] = total[:, p * TS : (p + 1) * TS]
-            return carry
-
-        lax.fori_loop(0, PARTS, stay, 0)
-        swap().wait_recv()
+        for h in (1, 0):
+            if h == 0:
+                for j in range(2):
+                    b_copy(3, j, True).wait_recv()
+                    b_copy(4, j, True).wait_recv()
+            send_partial(near, 2, h, h == 0)
+            part = product(near, 2, r, h, h == 0)
+
+            def stay(i, carry, part=part, h=h):
+                at, total = part(i)
+                for p in range(2):
+                    f_out[i, 2 * h + p] = total[:, p * TS : (p + 1) * TS]
+                return carry
+
+            lax.fori_loop(0, PARTS, stay, 0)
+        swap(1).wait_recv()
+        swap(0).wait_recv()
+
+        def place(i, p, extra):
+            value = f_out[i, p] + part_in[p // 2, rows(i), pl.ds((p % 2) * TS, TS)]
+            if extra:
+                value = value + f_in[i, p]
+            out_ref[rows(i), pl.ds(p * TS, TS)] = value.astype(jnp.bfloat16)
+
+        for i in range(PARTS):
+            place(i, 0, False)
         for i, p in FAR_ORDER:
             f_copy(i, p).wait_recv()
-            cols = pl.ds(p * TS, TS)
-            value = f_out[i, p] + part_in[rows(i), cols] + f_in[i, p]
-            out_ref[rows(i), cols] = value.astype(jnp.bfloat16)
-        for i in range(PARTS):
-            far_copy(0, i).wait_send()
+            place(i, p, True)
+        for i in range(PARTS):
+            for h in range(2):
+                far_copy(0, i, h).wait_send()
 
     @pl.when(inner)
     def _():
@@ -309,8 +329,13 @@
             b_copy(2, j).start()
 
         def far_pass(i):
-            far_copy(0, i, True).wait_recv()
-            far_copy(1, i).start()
+            for h in range(2):
+                far_copy(0, i, h, True).wait_recv()
+                far_copy(1, i, h).start()
+
+        def far_got(i):
+            for h in range(2):
+                far_copy(1, i, h, True).wait_recv()
 
         def far_b(p):
             for j in (2 * p, 2 * p + 1):
@@ -328,64 +353,79 @@
         pass_b(3)
         a_pass(1)
         a_own(3)
+        pass_b(4)
+        far_b(0)
+        for j in range(2):
+            b_copy(3, j).start()
+            b_copy(4, j).start()
         far_pass(0)
+        a_pass(2)
+        pass_b(5)
         far_pass(1)
-        a_pass(2)
-        pass_b(4)
-        pass_b(5)
-        far_copy(1, 0, True).wait_recv()
-        far_copy(1, 1, True).wait_recv()
-        far_b(0)
+        a_pass(3)
+        pass_b(6)
+        pass_b(7)
         far_b(1)
-        far_steps(FAR_ORDER[0:4])
-        a_pass(3)
-        far_pass(2)
-        pass_b(6)
+        far_got(0)
+        far_got(1)
+        far_steps(FAR_ORDER[0:2])
         far_b(2)
-        far_steps(FAR_ORDER[4:6])
-        far_pass(3)
-        pass_b(7)
-        far_copy(1, 2, True).wait_recv()
-        far_steps(FAR_ORDER[6:9])
-        far_copy(1, 3, True).wait_recv()
-        far_steps(FAR_ORDER[9:12])
-        far_b(3)
-        far_steps(FAR_ORDER[12:16])
+        far_steps(FAR_ORDER[2:4])
         for i in range(PARTS):
             a_done(i)
             for s in range(rows_n):
                 order(s, i)
-        send_partial(0, rows_n)
-        part = product(0, rows_n, r)
+        far_pass(2)
+        send_partial(0, rows_n, 0)
+        part = product(0, rows_n, r, 0)
 
         def keep(i, carry):
-            at, total = part(i)
-            for p in range(steps):
-                fp_out[i, p] = total[:, p * TS : (p + 1) * TS]
+            _, total = part(i)
+            fp_out[i, 0] = total[:, :TS]
+            f_out[i, 0] = total[:, TS:]
             return carry
 
+        lax.fori_loop(0, PARTS, keep, 0)
+        far_got(2)
+        far_steps(FAR_ORDER[4:6])
+        far_pass(3)
+        far_b(3)
+        far_steps(FAR_ORDER[6:9])
+        far_got(3)
+        far_steps(FAR_ORDER[9:12])
+        send_partial(0, rows_n, 1)
+        swap(0).wait_recv()
+        for i in range(PARTS):
+            for p in range(2):
+                own_part = (fp_out, f_out)[p][i, 0]
+                cols = pl.ds(p * TS, TS)
+                out_ref[rows(i), cols] = (own_part + part_in[0, rows(i), cols]).astype(
+                    jnp.bfloat16
+                )
+        swap(1).wait_recv()
+        part1 = product(0, rows_n, r, 1)
+
+        def stay(i, carry):
+            at, total = part1(i)
+            out_ref[at, pl.ds(wide, wide)] = (total + part_in[1, at, :]).astype(jnp.bfloat16)
+            return carry
+
+        lax.fori_loop(0, PARTS, stay, 0)
         for i, p in FAR_ORDER:
             fp_copy(i, p).wait_send()
-        lax.fori_loop(0, PARTS, keep, 0)
-        swap().wait_recv()
-
-        def stay(i, carry):
-            at = pl.ds(pl.multiple_of(i * ra, ra), ra)
-            for p in range(steps):
-                cols = pl.ds(p * TS, TS)
-                out_ref[at, cols] = (fp_out[i, p] + part_in[at, cols]).astype(jnp.bfloat16)
-            return carry
-
-        lax.fori_loop(0, PARTS, stay, 0)
-        for i, p in FAR_ORDER:
             f_copy(i, p).wait_send()
         for i in range(PARTS):
-            far_copy(1, i).wait_send()
+            for h in range(2):
+                far_copy(1, i, h).wait_send()
         for j in range(chunks):
             b_copy(1, j).wait_send()
             b_copy(2, j).wait_send()
-
-    swap().wait_send()
+        for j in range(2):
+            b_copy(3, j).wait_send()
+            b_copy(4, j).wait_send()
+
+    for h in range(2):
+        swap(h).wait_send()
     for i in range(PARTS):
         for kind in range(4):
             a_copy(kind, i).wait_send()
@@ -394,11 +434,10 @@
 
 
 FAR_ORDER = (
-    (0, 0), (1, 0), (0, 1), (1, 1),
-    (0, 2), (1, 2),
-    (2, 0), (2, 1), (2, 2),
-    (3, 0), (3, 1), (3, 2),
-    (0, 3), (1, 3), (2, 3), (3, 3),
+    (0, 1), (1, 1), (0, 2), (1, 2),
+    (2, 1), (2, 2),
+    (0, 3), (1, 3), (2, 3),
+    (3, 1), (3, 2), (3, 3),
 )
 
 
@@ -425,24 +464,24 @@
             pltpu.VMEM((rows_n, mrow, kb), jnp.bfloat16),
             pltpu.VMEM((2, mrow, kb), jnp.bfloat16),
             pltpu.VMEM((rows_n, kb, ncol), jnp.bfloat16),
-            pltpu.VMEM((mrow, half), jnp.float32),
-            pltpu.VMEM((mrow, half), jnp.float32),
+            pltpu.VMEM((2, mrow, half // 2), jnp.float32),
+            pltpu.VMEM((2, mrow, half // 2), jnp.float32),
             tiles,
             tiles,
             tiles,
             dma((PARTS, kcol // TS)),
             dma((4, PARTS)),
             dma((4, PARTS)),
-            dma((3, 2 * steps)),
-            dma((3, 2 * steps)),
-            dma((2, PARTS)),
-            dma((2, PARTS)),
+            dma((5, 2 * steps)),
+            dma((5, 2 * steps)),
+            dma((2, PARTS, 2)),
+            dma((2, PARTS, 2)),
             dma((PARTS, steps)),
             dma((PARTS, steps)),
             dma((PARTS, steps)),
             dma((PARTS, steps)),
-            dma((1,)),
-            dma((1,)),
+            dma((2,)),
+            dma((2,)),
         ],
         compiler_params=pltpu.CompilerParams(
             collective_id=0, has_side_effects=True, vmem_limit_bytes=56 << 20

time: 148 us -> 130 us (0.88)
  Pallas kernels: 144 us -> 126 us
    pallas_call x1, Pallas kernels: 144 us -> 126 us  [fused(): pl.pallas_call(kernel, out_shape=jax.ShapeDtypeStruct((mrow, half), jnp.b...]
where the time goes in v2:
time: 130 us
  Pallas kernels  126 us (97%)
  local copies, waits for them, and re-layouts  3.68 us (3%)
    pallas_call x1, Pallas kernels, fused(): pl.pallas_call(kernel, out_shape=jax.ShapeDtypeStruct((mrow, half), jnp.b...  126 us
    unnamed x2, local copies, waits for them, and re-layouts  3.68 us

profile of v2, /device:TPU:0, one launch (start us, length us, event | category | flops | bytes accessed | tf_op | source)
XLA Modules:
  0.0 129.8 jit_solution(16443055419348603408)
XLA Ops:
  0.0 1.4 %copy.7.mask_ref = s32[64,32]{1,0:T(8,128)} copy(s32[64,32]{0,1:T(8,128)} %param.8) | data formatting | bytes 16384 | tf_op args[2]
  1.4 126.1 %shard_map.64 = bf16[1024,512]{1,0:T(8,128)(2,1)} custom-call(bf16[1024,1024]{1,0:T(8,128)(2,1)} %a_ref.1, bf16[1024,1024]{1,0:T(8,128)(2,1)} %b_ref.1, s32[64,32]{1,0:T(8,128)} %copy.7.mask_ref, s32[64]{0:T(128)} %k_ref.1, s32[32]{0:T(128)} %n_ref.1, s32[64]{0:T(128)} %stored_ref.1), custom_call_target="tpu_custom_call" | custom-call | flops 8589934592 | bytes 5242880 | tf_op jit(solution)/shard_map/pallas_call | solution.py:454
  127.5 2.3 %copy.9 = bf16[1024,512]{1,0:T(8,128)(2,1)} copy(bf16[1024,512]{1,0:T(8,128)(2,1)} %shard_map.64) | data formatting | bytes 2097152

commit v3 on v2

--- a/solution.py
+++ b/solution.py
@@ -9,6 +9,7 @@
 
 TS = 128
 PARTS = 4
+SPLIT = 5
 
 
 def remote(src, dst, send_sem, recv_sem, **target):
@@ -34,6 +35,7 @@
     a_1,
     a_2,
     a_3,
+    a_4,
     a_ord,
     a_far,
     b_all,
@@ -42,6 +44,7 @@
     fp_out,
     f_in,
     f_out,
+    acc,
     own_sem,
     a_send,
     a_recv,
@@ -56,7 +59,7 @@
     p_send,
     p_recv,
 ):
-    a_all = (a_0, a_1, a_2, a_3)
+    a_all = (a_0, a_1, a_2, a_3, a_4)
     z = lax.axis_index("row")
     c = lax.axis_index("col")
     r = lax.axis_index("rep")
@@ -84,13 +87,22 @@
     wide = half // 2
     mesh_id = pl.DeviceIdType.MESH
 
+    def size(i):
+        return ra if i < PARTS - 1 else ra // 2
+
+    def start(i):
+        return i * ra if i < PARTS else i * ra - ra // 2
+
+    def rows(i):
+        return pl.ds(start(i), size(i))
+
     own = [
         pltpu.make_async_copy(
-            a_ref.at[pl.ds(i * ra, ra), pl.ds(t * TS, TS)],
+            a_ref.at[rows(i), pl.ds(t * TS, TS)],
             a_all[i].at[c * per + t],
             own_sem.at[i, t],
         )
-        for i in range(PARTS)
+        for i in range(SPLIT)
         for t in range(per)
     ]
     for copy in own:
@@ -105,14 +117,6 @@
     @pl.when(inner)
     def _():
         pl.semaphore_signal(barrier, inc=1, device_id={"row": across}, device_id_type=mesh_id)
-
-    pl.semaphore_wait(barrier, 4 + jnp.where(inner, 1, 0))
-
-    for copy in own:
-        copy.wait()
-
-    def rows(i):
-        return pl.ds(i * ra, ra)
 
     def a_copy(kind, i, receive=False):
         link = kind % 2
@@ -121,12 +125,12 @@
             view = a_all[i].at[pl.ds(owner * per, per)]
         else:
             owner = diag if receive else (yn, xn)[link]
-            part = pl.ds(link * (ra // 2), ra // 2)
+            part = pl.ds(link * (size(i) // 2), size(i) // 2)
             view = a_all[i].at[pl.ds(owner * per, per), part, :]
         return remote(view, view, a_send.at[kind, i], a_recv.at[kind, i], col=(xn, yn)[link])
 
     def a_own(i):
-        if i < PARTS:
+        if i < SPLIT:
             a_copy(0, i).start()
             a_copy(1, i).start()
 
@@ -158,7 +162,7 @@
 
     def far_copy(kind, i, h, receive=False):
         side = (x, y)[h]
-        at = pl.ds(i * ra + h * (ra // 2), ra // 2)
+        at = pl.ds(start(i) + h * (size(i) // 2), size(i) // 2)
         if kind == 0:
             src = a_far.at[side, at, :] if receive else a_ord.at[far + side, at, :]
             dst = a_far.at[side, at, :]
@@ -168,14 +172,17 @@
             view, view, far_send.at[1, i, h], far_recv.at[1, i, h], col=(xn, yn)[h]
         )
 
+    def piece(ref, i, p):
+        return ref.at[i, p, pl.ds(0, size(i))]
+
     def fp_copy(i, p):
         return remote(
-            fp_out.at[i, p], f_in.at[i, p], fp_send.at[i, p], fp_recv.at[i, p], rep=1 - r
+            piece(fp_out, i, p), piece(f_in, i, p), fp_send.at[i, p], fp_recv.at[i, p], rep=1 - r
         )
 
     def f_copy(i, p):
         return remote(
-            f_out.at[i, p], f_in.at[i, p], f_send.at[i, p], f_recv.at[i, p], row=buddy
+            piece(f_out, i, p), piece(f_in, i, p), f_send.at[i, p], f_recv.at[i, p], row=buddy
         )
 
     def swap(h):
@@ -195,7 +202,7 @@
 
         def one(t, carry):
             k = stored_ref[r * slab_tiles + z * slots + t]
-            ok = jnp.logical_and(k_ref[k] == n_ref[g], mask_ref[k, g] == 1)
+            ok = jnp.logical_and(k_ref[k] == n_ref[g], mask_ref[g, k] == 1)
             weight = jnp.where(ok, 1.0, 0.0).astype(jnp.float32)
             at = pl.ds(pl.multiple_of(t * TS, TS), TS)
             value = b_ref[at, lanes(tile)].astype(jnp.float32) * weight
@@ -241,7 +248,7 @@
         swap(h).start()
 
     def far_dot(i, j):
-        total = jnp.zeros((ra, TS), jnp.float32)
+        total = jnp.zeros((size(i), TS), jnp.float32)
         for s in range(2):
             total += jnp.dot(
                 a_far[s, rows(i), :],
@@ -252,26 +259,32 @@
 
     def far_steps(pairs):
         for i, p in pairs:
-            fp_out[i, p] = far_dot(i, 2 * p)
+            piece(fp_out, i, p)[...] = far_dot(i, 2 * p)
             fp_copy(i, p).start()
         for i, p in pairs:
             total = far_dot(i, 2 * p + 1)
             fp_copy(i, p).wait_recv()
-            f_out[i, p] = total + f_in[i, p]
+            piece(f_out, i, p)[...] = total + piece(f_in, i, p)[...]
             f_copy(i, p).start()
 
+    chunks = 2 * steps
+    for j in range(PARTS):
+        mask(j)
+    pl.semaphore_wait(barrier, 4 + jnp.where(inner, 1, 0))
+    for j in range(PARTS):
+        b_copy(0, j).start()
+    for copy in own:
+        copy.wait()
     a_own(0)
     a_own(1)
-    chunks = 2 * steps
+    for j in range(PARTS, chunks):
+        mask(j)
 
     @pl.when(end)
     def _():
         sent = PARTS + 1
-        for j in range(chunks):
-            mask(j)
-            if j < sent:
-                b_copy(0, j).start()
-        for i in range(PARTS):
+        b_copy(0, PARTS).start()
+        for i in range(SPLIT):
             a_pass(i)
             a_own(i + 2)
             a_done(i)
@@ -283,7 +296,7 @@
             for j in range(sent, upto):
                 b_copy(0, j).start()
             sent = upto
-        for i in range(PARTS):
+        for i in range(SPLIT):
             order(near, i)
             order(near + 1, i)
         for j in range(chunks):
@@ -298,8 +311,7 @@
 
             def stay(i, carry, part=part, h=h):
                 at, total = part(i)
-                for p in range(2):
-                    f_out[i, 2 * h + p] = total[:, p * TS : (p + 1) * TS]
+                acc[at, pl.ds(h * wide, wide)] = total
                 return carry
 
             lax.fori_loop(0, PARTS, stay, 0)
@@ -307,17 +319,18 @@
         swap(0).wait_recv()
 
         def place(i, p, extra):
-            value = f_out[i, p] + part_in[p // 2, rows(i), pl.ds((p % 2) * TS, TS)]
+            value = acc[rows(i), pl.ds(p * TS, TS)]
+            value = value + part_in[p // 2, rows(i), pl.ds((p % 2) * TS, TS)]
             if extra:
-                value = value + f_in[i, p]
+                value = value + piece(f_in, i, p)[...]
             out_ref[rows(i), pl.ds(p * TS, TS)] = value.astype(jnp.bfloat16)
 
-        for i in range(PARTS):
+        for i in range(SPLIT):
             place(i, 0, False)
         for i, p in FAR_ORDER:
             f_copy(i, p).wait_recv()
             place(i, p, True)
-        for i in range(PARTS):
+        for i in range(SPLIT):
             for h in range(2):
                 far_copy(0, i, h).wait_send()
 
@@ -342,8 +355,7 @@
                 b_copy(1, j, True).wait_recv()
                 b_copy(2, j, True).wait_recv()
 
-        for j in range(chunks):
-            mask(j)
+        for j in range(PARTS, chunks):
             b_copy(0, j).start()
         pass_b(0)
         pass_b(1)
@@ -360,9 +372,11 @@
             b_copy(4, j).start()
         far_pass(0)
         a_pass(2)
+        a_own(4)
         pass_b(5)
         far_pass(1)
         a_pass(3)
+        a_pass(4)
         pass_b(6)
         pass_b(7)
         far_b(1)
@@ -371,7 +385,7 @@
         far_steps(FAR_ORDER[0:2])
         far_b(2)
         far_steps(FAR_ORDER[2:4])
-        for i in range(PARTS):
+        for i in range(SPLIT):
             a_done(i)
             for s in range(rows_n):
                 order(s, i)
@@ -380,9 +394,8 @@
         part = product(0, rows_n, r, 0)
 
         def keep(i, carry):
-            _, total = part(i)
-            fp_out[i, 0] = total[:, :TS]
-            f_out[i, 0] = total[:, TS:]
+            at, total = part(i)
+            acc[at, pl.ds(0, wide)] = total
             return carry
 
         lax.fori_loop(0, PARTS, keep, 0)
@@ -393,15 +406,12 @@
         far_steps(FAR_ORDER[6:9])
         far_got(3)
         far_steps(FAR_ORDER[9:12])
+        far_pass(4)
+        far_got(4)
+        far_steps(FAR_ORDER[12:15])
         send_partial(0, rows_n, 1)
         swap(0).wait_recv()
-        for i in range(PARTS):
-            for p in range(2):
-                own_part = (fp_out, f_out)[p][i, 0]
-                cols = pl.ds(p * TS, TS)
-                out_ref[rows(i), cols] = (own_part + part_in[0, rows(i), cols]).astype(
-                    jnp.bfloat16
-                )
+        out_ref[:, :wide] = (acc[:, :wide] + part_in[0]).astype(jnp.bfloat16)
         swap(1).wait_recv()
         part1 = product(0, rows_n, r, 1)
 
@@ -414,7 +424,7 @@
         for i, p in FAR_ORDER:
             fp_copy(i, p).wait_send()
             f_copy(i, p).wait_send()
-        for i in range(PARTS):
+        for i in range(SPLIT):
             for h in range(2):
                 far_copy(1, i, h).wait_send()
         for j in range(chunks):
@@ -426,7 +436,7 @@
 
     for h in range(2):
         swap(h).wait_send()
-    for i in range(PARTS):
+    for i in range(SPLIT):
         for kind in range(4):
             a_copy(kind, i).wait_send()
     for j in range(chunks):
@@ -438,6 +448,7 @@
     (2, 1), (2, 2),
     (0, 3), (1, 3), (2, 3),
     (3, 1), (3, 2), (3, 3),
+    (4, 1), (4, 2), (4, 3),
 )
 
 
@@ -448,8 +459,9 @@
     steps = half // TS
     smem = pl.BlockSpec(memory_space=pltpu.SMEM)
     vmem = pl.BlockSpec(memory_space=pltpu.VMEM)
-    tiles = pltpu.VMEM((PARTS, steps, mrow // PARTS, TS), jnp.float32)
+    tiles = pltpu.VMEM((SPLIT, steps, mrow // PARTS, TS), jnp.float32)
     chunk = pltpu.VMEM((cols_n * kcol // TS, mrow // PARTS, TS), jnp.bfloat16)
+    last = pltpu.VMEM((cols_n * kcol // TS, mrow // PARTS // 2, TS), jnp.bfloat16)
     dma = pltpu.SemaphoreType.DMA
     return pl.pallas_call(
         kernel,
@@ -460,7 +472,8 @@
             chunk,
             chunk,
             chunk,
-            chunk,
+            last,
+            last,
             pltpu.VMEM((rows_n, mrow, kb), jnp.bfloat16),
             pltpu.VMEM((2, mrow, kb), jnp.bfloat16),
             pltpu.VMEM((rows_n, kb, ncol), jnp.bfloat16),
@@ -469,17 +482,18 @@
             tiles,
             tiles,
             tiles,
-            dma((PARTS, kcol // TS)),
-            dma((4, PARTS)),
-            dma((4, PARTS)),
+            pltpu.VMEM((mrow, half), jnp.float32),
+            dma((SPLIT, kcol // TS)),
+            dma((4, SPLIT)),
+            dma((4, SPLIT)),
             dma((5, 2 * steps)),
             dma((5, 2 * steps)),
-            dma((2, PARTS, 2)),
-            dma((2, PARTS, 2)),
-            dma((PARTS, steps)),
-            dma((PARTS, steps)),
-            dma((PARTS, steps)),
-            dma((PARTS, steps)),
+            dma((2, SPLIT, 2)),
+            dma((2, SPLIT, 2)),
+            dma((SPLIT, steps)),
+            dma((SPLIT, steps)),
+            dma((SPLIT, steps)),
+            dma((SPLIT, steps)),
             dma((2,)),
             dma((2,)),
         ],
@@ -491,7 +505,7 @@
             bytes_accessed=2 * (mrow * kcol + kb * ncol + mrow * half),
             transcendentals=0,
         ),
-    )(amplitudes, integrals, tile_mask, k_irrep, n_irrep, stored_tile)
+    )(amplitudes, integrals, tile_mask.T, k_irrep, n_irrep, stored_tile)
 
 
 def gathered_form(amplitudes, integrals, tile_mask, k_irrep, n_irrep, stored_tile):

time: 130 us -> 129 us (level)
  local copies, waits for them, and re-layouts: 3.68 us -> 2.26 us
    unnamed x2 -> x1, local copies, waits for them, and re-layouts: 3.68 us -> 2.26 us
where the time goes in v3:
time: 129 us
  Pallas kernels  127 us (98%)
  local copies, waits for them, and re-layouts  2.26 us (2%)
    pallas_call x1, Pallas kernels, fused(): pl.pallas_call(kernel, out_shape=jax.ShapeDtypeStruct((mrow, half), jnp.b...  127 us

profile of v3, /device:TPU:0, one launch (start us, length us, event | category | flops | bytes accessed | tf_op | source)
XLA Modules:
  0.0 129.3 jit_solution(5870077996717389711)
XLA Ops:
  0.0 127.0 %shard_map.64 = bf16[1024,512]{1,0:T(8,128)(2,1)} custom-call(bf16[1024,1024]{1,0:T(8,128)(2,1)} %a_ref.1, bf16[1024,1024]{1,0:T(8,128)(2,1)} %b_ref.1, s32[32,64]{1,0:T(8,128)} %bitcast.1, s32[64]{0:T(128)} %k_ref.1, s32[32]{0:T(128)} %n_ref.1, s32[64]{0:T(128)} %stored_ref.1), custom_call_target="tpu_custom_call" | custom-call | flops 8589934592 | bytes 5242880 | tf_op jit(solution)/shard_map/pallas_call | solution.py:466
  127.0 2.3 %copy.8 = bf16[1024,512]{1,0:T(8,128)(2,1)} copy(bf16[1024,512]{1,0:T(8,128)(2,1)} %shard_map.64) | data formatting | bytes 2097152

commit v4 on v3

--- a/solution.py
+++ b/solution.py
@@ -211,7 +211,7 @@
 
         lax.fori_loop(0, slots, one, 0)
 
-    def product(first, count, side, h, extra=False):
+    def product(first, count, side, h):
         cols = pl.ds(pl.multiple_of(side * half + h * wide, wide), wide)
 
         def one(i):
@@ -223,21 +223,12 @@
                     b_all[first + s, :, cols],
                     preferred_element_type=jnp.float32,
                 )
-            if not extra:
-                return at, total
-            more = jnp.zeros((ra, TS), jnp.float32)
-            for s in range(2):
-                more += jnp.dot(
-                    a_ord[far + s, at, :],
-                    b_all[far + s, :, lanes(side * steps)],
-                    preferred_element_type=jnp.float32,
-                )
-            return at, jnp.concatenate([total[:, :TS] + more, total[:, TS:]], axis=1)
+            return at, total
 
         return one
 
-    def send_partial(first, count, h, extra=False):
-        part = product(first, count, 1 - r, h, extra)
+    def send_partial(first, count, h):
+        part = product(first, count, 1 - r, h)
 
         def away(i, carry):
             at, total = part(i)
@@ -282,8 +273,9 @@
 
     @pl.when(end)
     def _():
-        sent = PARTS + 1
+        sent = PARTS + 2
         b_copy(0, PARTS).start()
+        b_copy(0, PARTS + 1).start()
         for i in range(SPLIT):
             a_pass(i)
             a_own(i + 2)
@@ -292,7 +284,7 @@
             order(far + 1, i)
             for h in range(2):
                 far_copy(0, i, h).start()
-            upto = min(chunks, sent + i + 1)
+            upto = min(chunks, sent + 2)
             for j in range(sent, upto):
                 b_copy(0, j).start()
             sent = upto
@@ -303,11 +295,12 @@
             b_copy(0, j, True).wait_recv()
         for h in (1, 0):
             if h == 0:
-                for j in range(2):
+                for j in range(PARTS):
                     b_copy(3, j, True).wait_recv()
                     b_copy(4, j, True).wait_recv()
-            send_partial(near, 2, h, h == 0)
-            part = product(near, 2, r, h, h == 0)
+            first, count = (0, rows_n) if h == 0 else (near, 2)
+            send_partial(first, count, h)
+            part = product(first, count, r, h)
 
             def stay(i, carry, part=part, h=h):
                 at, total = part(i)
@@ -327,6 +320,7 @@
 
         for i in range(SPLIT):
             place(i, 0, False)
+            place(i, 1, False)
         for i, p in FAR_ORDER:
             f_copy(i, p).wait_recv()
             place(i, p, True)
@@ -345,6 +339,11 @@
             for h in range(2):
                 far_copy(0, i, h, True).wait_recv()
                 far_copy(1, i, h).start()
+
+        def raw(p):
+            for j in (2 * p, 2 * p + 1):
+                b_copy(3, j).start()
+                b_copy(4, j).start()
 
         def far_got(i):
             for h in range(2):
@@ -367,29 +366,22 @@
         a_own(3)
         pass_b(4)
         far_b(0)
-        for j in range(2):
-            b_copy(3, j).start()
-            b_copy(4, j).start()
-        far_pass(0)
+        raw(0)
+        pass_b(5)
         a_pass(2)
         a_own(4)
-        pass_b(5)
-        far_pass(1)
+        far_b(1)
+        raw(1)
+        far_pass(0)
         a_pass(3)
-        a_pass(4)
         pass_b(6)
         pass_b(7)
-        far_b(1)
-        far_got(0)
-        far_got(1)
-        far_steps(FAR_ORDER[0:2])
-        far_b(2)
-        far_steps(FAR_ORDER[2:4])
+        a_pass(4)
         for i in range(SPLIT):
             a_done(i)
             for s in range(rows_n):
                 order(s, i)
-        far_pass(2)
+        far_pass(1)
         send_partial(0, rows_n, 0)
         part = product(0, rows_n, r, 0)
 
@@ -399,16 +391,20 @@
             return carry
 
         lax.fori_loop(0, PARTS, keep, 0)
+        far_b(2)
+        far_got(0)
+        far_got(1)
+        far_steps(FAR_ORDER[0:2])
+        far_pass(2)
+        far_pass(3)
         far_got(2)
-        far_steps(FAR_ORDER[4:6])
-        far_pass(3)
+        far_steps(FAR_ORDER[2:3])
+        far_pass(4)
         far_b(3)
-        far_steps(FAR_ORDER[6:9])
+        far_steps(FAR_ORDER[3:6])
         far_got(3)
-        far_steps(FAR_ORDER[9:12])
-        far_pass(4)
         far_got(4)
-        far_steps(FAR_ORDER[12:15])
+        far_steps(FAR_ORDER[6:10])
         send_partial(0, rows_n, 1)
         swap(0).wait_recv()
         out_ref[:, :wide] = (acc[:, :wide] + part_in[0]).astype(jnp.bfloat16)
@@ -430,7 +426,7 @@
         for j in range(chunks):
             b_copy(1, j).wait_send()
             b_copy(2, j).wait_send()
-        for j in range(2):
+        for j in range(PARTS):
             b_copy(3, j).wait_send()
             b_copy(4, j).wait_send()
 
@@ -444,11 +440,9 @@
 
 
 FAR_ORDER = (
-    (0, 1), (1, 1), (0, 2), (1, 2),
-    (2, 1), (2, 2),
+    (0, 2), (1, 2), (2, 2),
     (0, 3), (1, 3), (2, 3),
-    (3, 1), (3, 2), (3, 3),
-    (4, 1), (4, 2), (4, 3),
+    (3, 2), (3, 3), (4, 2), (4, 3),
 )
 
 

time: 129 us -> 125 us (0.969)
  Pallas kernels: 127 us -> 123 us
    pallas_call x1, Pallas kernels: 127 us -> 123 us  [fused(): pl.pallas_call(kernel, out_shape=jax.ShapeDtypeStruct((mrow, half), jnp.b...]
where the time goes in v4:
time: 125 us
  Pallas kernels  123 us (98%)
  local copies, waits for them, and re-layouts  2.26 us (2%)
    pallas_call x1, Pallas kernels, fused(): pl.pallas_call(kernel, out_shape=jax.ShapeDtypeStruct((mrow, half), jnp.b...  123 us

profile of v4, /device:TPU:0, one launch (start us, length us, event | category | flops | bytes accessed | tf_op | source)
XLA Modules:
  0.0 125.1 jit_solution(6655713725148633596)
XLA Ops:
  0.0 122.9 %shard_map.64 = bf16[1024,512]{1,0:T(8,128)(2,1)} custom-call(bf16[1024,1024]{1,0:T(8,128)(2,1)} %a_ref.1, bf16[1024,1024]{1,0:T(8,128)(2,1)} %b_ref.1, s32[32,64]{1,0:T(8,128)} %bitcast.1, s32[64]{0:T(128)} %k_ref.1, s32[32]{0:T(128)} %n_ref.1, s32[64]{0:T(128)} %stored_ref.1), custom_call_target="tpu_custom_call" | custom-call | flops 8589934592 | bytes 5242880 | tf_op jit(solution)/shard_map/pallas_call | solution.py:460
  122.9 2.3 %copy.8 = bf16[1024,512]{1,0:T(8,128)(2,1)} copy(bf16[1024,512]{1,0:T(8,128)(2,1)} %shard_map.64) | data formatting | bytes 2097152

commit v5 on v4

--- a/solution.py
+++ b/solution.py
@@ -248,10 +248,12 @@
             )
         return total
 
-    def far_steps(pairs):
+    def far_away(pairs):
         for i, p in pairs:
             piece(fp_out, i, p)[...] = far_dot(i, 2 * p)
             fp_copy(i, p).start()
+
+    def far_back(pairs):
         for i, p in pairs:
             total = far_dot(i, 2 * p + 1)
             fp_copy(i, p).wait_recv()
@@ -394,17 +396,22 @@
         far_b(2)
         far_got(0)
         far_got(1)
-        far_steps(FAR_ORDER[0:2])
+        far_away(FAR_ORDER[0:2])
+        far_back(FAR_ORDER[0:2])
         far_pass(2)
         far_pass(3)
         far_got(2)
-        far_steps(FAR_ORDER[2:3])
+        far_away(FAR_ORDER[2:3])
+        far_back(FAR_ORDER[2:3])
         far_pass(4)
         far_b(3)
-        far_steps(FAR_ORDER[3:6])
+        far_away(FAR_ORDER[3:6])
         far_got(3)
+        far_away(FAR_ORDER[6:8])
+        far_back(FAR_ORDER[3:6])
         far_got(4)
-        far_steps(FAR_ORDER[6:10])
+        far_away(FAR_ORDER[8:10])
+        far_back(FAR_ORDER[6:10])
         send_partial(0, rows_n, 1)
         swap(0).wait_recv()
         out_ref[:, :wide] = (acc[:, :wide] + part_in[0]).astype(jnp.bfloat16)

time: 125 us -> 125 us (level)
  no operation moved by 1% of the time
where the time goes in v5:
time: 125 us
  Pallas kernels  123 us (98%)
  local copies, waits for them, and re-layouts  2.26 us (2%)
    pallas_call x1, Pallas kernels, fused(): pl.pallas_call(kernel, out_shape=jax.ShapeDtypeStruct((mrow, half), jnp.b...  123 us

profile of v5, /device:TPU:0, one launch (start us, length us, event | category | flops | bytes accessed | tf_op | source)
XLA Modules:
  0.0 125.1 jit_solution(1820882602789609554)
XLA Ops:
  0.0 122.9 %shard_map.64 = bf16[1024,512]{1,0:T(8,128)(2,1)} custom-call(bf16[1024,1024]{1,0:T(8,128)(2,1)} %a_ref.1, bf16[1024,1024]{1,0:T(8,128)(2,1)} %b_ref.1, s32[32,64]{1,0:T(8,128)} %bitcast.1, s32[64]{0:T(128)} %k_ref.1, s32[32]{0:T(128)} %n_ref.1, s32[64]{0:T(128)} %stored_ref.1), custom_call_target="tpu_custom_call" | custom-call | flops 8589934592 | bytes 5242880 | tf_op jit(solution)/shard_map/pallas_call | solution.py:467
  122.9 2.3 %copy.8 = bf16[1024,512]{1,0:T(8,128)(2,1)} copy(bf16[1024,512]{1,0:T(8,128)(2,1)} %shard_map.64) | data formatting | bytes 2097152
